TPU v7x, 32 devices: a whole 2x2x4 slice. The times are simulated.
32 devices in a mesh: serve: 2 (over x), store: 16 (over z, y, core).
Axes of the slice: x: 2, y: 2, z: 4, core: 2. Of those that a mesh axis runs over, the one named last changes fastest.
Arguments:
- normalized_hidden_states: bfloat16 [16384, 2048], P(('serve', 'store')), may hold values from -20 to 20
- query_weight_matrix: bfloat16 [2048, 2048], replicated, may hold values from -0.125 to 0.125
- key_weight_matrix: bfloat16 [2048, 512], replicated, may hold values from -0.125 to 0.125
- value_weight_matrix: bfloat16 [2048, 512], replicated, may hold values from -0.125 to 0.125
- adapter_down_weight: bfloat16 [512, 32, 2048], P('store', None, 'serve'), may hold values from -0.125 to 0.125
- adapter_up_query_weight: bfloat16 [512, 16, 2048], P('store', None, 'serve'), may hold values from -1.5 to 1.5
- adapter_up_value_weight: bfloat16 [512, 16, 512], P('store', None, 'serve'), may hold values from -1.5 to 1.5
- adapter_panel_slot: int32 [512], replicated, may hold values from 0 to 511, as said below
- adapter_per_request: int32 [32, 16], P(('serve', 'store')), may hold values from 0 to 511, as said below
- request_token_length: int32 [32, 16], P(('serve', 'store')), may hold values from 1 to 64, 512 in all within a row
Outputs:
- attended: bfloat16 [16384, 2048], P(('serve', 'store'))
Inputs may be any that keep to these rules, and one draw needn't show every extreme that they name: Each number appears once; adapter a's panels are entry adapter_panel_slot[a] of the three panel arrays, whose owner is index adapter_panel_slot[a] // 32 of store. `adapter_per_request`: the 16 requests of one device use adapters of 16 different owners. `request_token_length`: each row sums to 512; the longest request of each device has exactly 64 tokens.
All inputs are finite; a program needn't handle non-finite values.
Results may differ from a plain program's by a relative error of at most 0.012.
Values may be sent and summed in bfloat16 or wider, within the bound.
A program may use at most 128 MiB of HBM per device.

v0:
```python
import jax
import jax.numpy as jnp
from jax import lax
from jax.sharding import PartitionSpec as P

HEADS = 32
KV_HEADS = 8
HEAD_DIM = 64
ADAPTER_RANK = 16
ADP_DEV = 32
LEN_MAX = 64


def rotary(heads_in, positions):
    half_dim = HEAD_DIM // 2
    frequency = 500000.0 ** (-(jnp.arange(half_dim).astype(jnp.float32) * 2.0 / HEAD_DIM))
    angles = positions.astype(jnp.float32)[:, None] * frequency[None, :]
    cosine_table = jnp.cos(angles)[:, None, :]
    sine_table = jnp.sin(angles)[:, None, :]
    first_half = heads_in[..., :half_dim]
    second_half = heads_in[..., half_dim:]
    return jnp.concatenate(
        [
            first_half * cosine_table - second_half * sine_table,
            second_half * cosine_table + first_half * sine_table,
        ],
        axis=-1,
    )


def table_lookup(table, wanted):
    entries = jnp.arange(table.shape[0], dtype=jnp.int32)
    return jnp.sum(jnp.where(wanted[..., None] == entries, table, 0), axis=-1)


def reduced_rank_products(block_list, down_panels, up_query, up_value):
    low = jnp.einsum(
        "jkd,jrd->jkr", block_list, down_panels, preferred_element_type=jnp.float32
    ).astype(jnp.bfloat16)
    query_update = jnp.einsum(
        "jkr,jrd->jkd", low[..., :ADAPTER_RANK], up_query, preferred_element_type=jnp.float32
    ).astype(jnp.bfloat16)
    value_update = jnp.einsum(
        "jkr,jrd->jkd", low[..., ADAPTER_RANK:], up_value, preferred_element_type=jnp.float32
    ).astype(jnp.bfloat16)
    return (query_update, value_update)


def local_choice(panel_set, lists, adapter_panel_slot, my_store):
    source_slots = table_lookup(adapter_panel_slot, lists)
    mine_mask = source_slots // ADP_DEV == my_store
    local_source = jnp.sum(jnp.where(mine_mask, source_slots % ADP_DEV, 0), axis=1)
    return tuple((jnp.take(panel, local_source, axis=0) for panel in panel_set))


def attention(query_rot, key_rot, value_rows, request_ids):
    tok_rows = query_rot.shape[0]
    per_group = HEADS // KV_HEADS
    block_rows = min(128, tok_rows)
    reach = LEN_MAX
    key_pad = jnp.concatenate(
        [jnp.zeros((reach,) + key_rot.shape[1:], key_rot.dtype), key_rot], axis=0
    )
    value_pad = jnp.concatenate(
        [jnp.zeros((reach,) + value_rows.shape[1:], value_rows.dtype), value_rows], axis=0
    )
    ids_pad = jnp.concatenate([jnp.full((reach,), -1, jnp.int32), request_ids], axis=0)
    token_order = jnp.arange(tok_rows, dtype=jnp.int32)
    order_pad = jnp.concatenate([jnp.full((reach,), -1, jnp.int32), token_order], axis=0)
    outputs = []
    for block_index in range(tok_rows // block_rows):
        first = block_index * block_rows
        query_block = query_rot[first : first + block_rows]
        query_ids = request_ids[first : first + block_rows]
        query_order = token_order[first : first + block_rows]
        key_block = key_pad[first : first + reach + block_rows]
        value_block = value_pad[first : first + reach + block_rows]
        key_ids = ids_pad[first : first + reach + block_rows]
        key_order = order_pad[first : first + reach + block_rows]
        allowed = (query_ids[:, None] == key_ids[None, :]) & (
            key_order[None, :] <= query_order[:, None]
        )
        pieces = []
        for group_index in range(KV_HEADS):
            query_part = query_block[:, group_index * per_group : (group_index + 1) * per_group, :]
            key_part = key_block[:, group_index, :]
            value_part = value_block[:, group_index, :]
            scores = jnp.einsum(
                "qhd,kd->hqk", query_part, key_part, preferred_element_type=jnp.float32
            ) * HEAD_DIM ** (-0.5)
            scores = jnp.where(allowed[None], scores, -jnp.inf)
            row_max = jnp.max(scores, axis=-1, keepdims=True)
            raised = jnp.exp(scores - row_max)
            row_total = jnp.sum(raised, axis=-1)
            weights = raised.astype(jnp.bfloat16)
            mixed_heads = (
                jnp.einsum("hqk,kd->qhd", weights, value_part, preferred_element_type=jnp.float32)
                / jnp.transpose(row_total)[:, :, None]
            )
            pieces.append(mixed_heads)
        outputs.append(
            jnp.concatenate(pieces, axis=1)
            .reshape(block_rows, HEADS * HEAD_DIM)
            .astype(jnp.bfloat16)
        )
    return jnp.concatenate(outputs, axis=0)


def local(
    normalized_hidden_states,
    query_weight_matrix,
    key_weight_matrix,
    value_weight_matrix,
    adapter_down_weight,
    adapter_up_query_weight,
    adapter_up_value_weight,
    adapter_panel_slot,
    adapter_per_request,
    request_token_length,
):
    store_count = lax.axis_size("store")
    my_store = lax.axis_index("store")
    tok_rows = normalized_hidden_states.shape[0]
    request_count = request_token_length.shape[1]
    group_lists = lax.all_gather(adapter_per_request, "store", axis=0, tiled=True)
    lengths = request_token_length[0]
    adapters = adapter_per_request[0]
    request_ends = jnp.cumsum(lengths)
    starts = request_ends - lengths
    token_order = jnp.arange(tok_rows, dtype=jnp.int32)
    request_ids = jnp.sum((token_order[:, None] >= request_ends[None, :]).astype(jnp.int32), axis=1)
    member = request_ids[:, None] == jnp.arange(request_count, dtype=jnp.int32)[None, :]
    positions = token_order - jnp.sum(jnp.where(member, starts[None, :], 0), axis=1)
    slot_index_list = table_lookup(adapter_panel_slot, adapters)
    owners = slot_index_list // ADP_DEV
    owner_pick = owners[None, :] == jnp.arange(store_count, dtype=jnp.int32)[:, None]
    start_for = jnp.sum(jnp.where(owner_pick, starts[None, :], 0), axis=1)
    length_for = jnp.sum(jnp.where(owner_pick, lengths[None, :], 0), axis=1)
    offsets = jnp.arange(LEN_MAX, dtype=jnp.int32)
    valid_rows = offsets[None, :] < length_for[:, None]
    row_index = jnp.where(valid_rows, start_for[:, None] + offsets[None, :], 0)
    block_list = jnp.where(
        valid_rows[..., None], normalized_hidden_states[row_index], jnp.zeros((), jnp.bfloat16)
    )
    owner_token = jnp.sum(jnp.where(member, owners[None, :], 0), axis=1)
    back_index = owner_token * LEN_MAX + positions
    panels = (
        lax.all_gather(adapter_down_weight, "serve", axis=2, tiled=True),
        lax.all_gather(adapter_up_query_weight, "serve", axis=2, tiled=True),
        lax.all_gather(adapter_up_value_weight, "serve", axis=2, tiled=True),
    )
    down_chosen, upq_chosen, upv_chosen = local_choice(
        panels, group_lists, adapter_panel_slot, my_store
    )
    arrived = lax.all_to_all(block_list, "store", split_axis=0, concat_axis=0, tiled=True)
    query_update, value_update = reduced_rank_products(arrived, down_chosen, upq_chosen, upv_chosen)
    query_update, value_update = (
        lax.all_to_all(query_update, "store", split_axis=0, concat_axis=0, tiled=True),
        lax.all_to_all(value_update, "store", split_axis=0, concat_axis=0, tiled=True),
    )
    delta_query = query_update.reshape(-1, query_update.shape[2])[back_index]
    delta_value = value_update.reshape(-1, value_update.shape[2])[back_index]
    base_query = jnp.dot(
        normalized_hidden_states, query_weight_matrix, preferred_element_type=jnp.float32
    ) + delta_query.astype(jnp.float32)
    query_rot = rotary(base_query.reshape(tok_rows, HEADS, HEAD_DIM), positions).astype(
        jnp.bfloat16
    )
    base_key = jnp.dot(
        normalized_hidden_states, key_weight_matrix, preferred_element_type=jnp.float32
    )
    key_rot = rotary(base_key.reshape(tok_rows, KV_HEADS, HEAD_DIM), positions).astype(jnp.bfloat16)
    value_rows = (
        jnp.dot(normalized_hidden_states, value_weight_matrix, preferred_element_type=jnp.float32)
        + delta_value.astype(jnp.float32)
    ).astype(jnp.bfloat16)
    value_rows = value_rows.reshape(tok_rows, KV_HEADS, HEAD_DIM)
    return attention(query_rot, key_rot, value_rows, request_ids)


def solution(mesh):
    return jax.shard_map(
        local,
        mesh=mesh,
        in_specs=(
            P(("serve", "store"), None),
            P(),
            P(),
            P(),
            P("store", None, "serve"),
            P("store", None, "serve"),
            P("store", None, "serve"),
            P(),
            P(("serve", "store"), None),
            P(("serve", "store"), None),
        ),
        out_specs=P(("serve", "store"), None),
        check_vma=False,
    )
```

profile of v0, /device:TPU:15, one launch (start us, length us, event | category | flops | bytes accessed | tf_op | source)
XLA Modules:
  0.0 365.0 jit_solution(15653382966586995664)
XLA Ops:
  10.1 6.0 %gather_fusion = bf16[1024,2048]{1,0:T(8,128)(2,1)} fusion(bf16[512,2048]{1,0:T(8,128)(2,1)S(1)} %copy-done, s32[1024]{0:T(1024)S(1)} %broadcast_clamp_fusion), kind=kCustom, calls=%fused_computation | custom fusion | bytes 8392704 | tf_op jit(solution)/shard_map/gather | solution.py:143
  16.1 4.5 %broadcast_select_fusion = bf16[16,64,2048]{2,1,0:T(8,128)(2,1)} fusion(bf16[16,64,2048]{2,1,0:T(8,128)(2,1)} %bitcast.784, pred[16,64]{1,0:T(8,128)(4,1)S(1)} %iota_compare_fusion.6), kind=kLoop, calls=%fused_computation.69 | loop fusion | flops 2097152 | bytes 8389632 | tf_op jit(solution)/shard_map/jit(_where)/select_n | solution.py:142
  20.6 6.6 %all-to-all-start = ((bf16[16,64,2048]{2,1,0:T(8,128)(2,1)}), bf16[16,64,2048]{2,1,0:T(8,128)(2,1)}, u32[]{:S(2)}, u32[]{:S(2)}) async-start(bf16[16,64,2048]{2,1,0:T(8,128)(2,1)} %broadcast_select_fusion), calls=%async_computation | async-start | bytes 8388608 | tf_op jit(solution)/shard_map/all_to_all | solution.py:155
  28.7 100.2 %all-gather = s32[16,1,16]{2,1,0:T(1,128)S(1)} all-gather(s32[1,1,16]{2,1,0:T(1,128)S(1)} %bitcast.854), channel_id=1, replica_groups=mesh['serve'=2,'store'=16] {'store'}, dimensions={0}, use_global_device_ids=true | all-gather | bytes 1088 | tf_op jit(solution)/shard_map/all_gather | solution.py:125
  129.5 8.4 %all_gather.14 = bf16[32,16,512]{2,1,0:T(8,128)(2,1)S(1)} all-gather(bf16[32,16,256]{2,1,0:T(8,128)(2,1)S(1)} %copy-done.29), channel_id=1, replica_groups=mesh['serve'=2,'store'=16] {'serve'}, dimensions={2}, use_global_device_ids=true | all-gather | bytes 786432 | tf_op jit(solution)/shard_map/all_gather | solution.py:150
  138.5 4.2 %gather_fusion.1 = bf16[16,32,2048]{2,1,0:T(8,128)(2,1)} fusion(bf16[32,32,2048]{2,1,0:T(8,128)(2,1)} %all-gather.4.cloned.1.call-done, s32[1024]{0:T(1024)S(1)} %pad_clamp_fusion.1), kind=kCustom, calls=%fused_computation.1 | custom fusion | bytes 4194368 | tf_op jit(solution)/shard_map/jit(_take)/gather | solution.py:53
  142.7 4.1 %fusion.68 = bf16[16,64,32]{1,2,0:T(8,128)(2,1)S(1)} fusion(bf16[16,64,2048]{2,1,0:T(8,128)(2,1)} %all-to-all-done, bf16[16,32,2048]{2,1,0:T(8,128)(2,1)} %gather_fusion.1, pred[16]{0:T(512)(128)(4,1)S(1)} %compare_and_fusion.4), kind=kOutput, calls=%fused_computation.225 | convolution fusion | flops 135299072 | bytes 6357008 | tf_op jit(solution)/shard_map/jkd,jrd->jkr/dot_general | solution.py:37
  148.3 5.8 %all-to-all-start.1 = ((bf16[16,64,512]{2,1,0:T(8,128)(2,1)}), bf16[16,64,512]{2,1,0:T(8,128)(2,1)}, u32[]{:S(2)}, u32[]{:S(2)}) async-start(bf16[16,64,512]{2,1,0:T(8,128)(2,1)} %convolution_convert_fusion.1), calls=%async_computation.1 | async-start | bytes 2097152 | tf_op jit(solution)/shard_map/all_to_all | solution.py:159
  154.1 3.2 gather_fusion.4
  157.3 4.5 %convolution_convert_fusion = bf16[16,64,2048]{2,1,0:T(8,128)(2,1)} fusion(bf16[16,16,2048]{2,1,0:T(8,128)(2,1)} %gather_fusion.4, pred[16]{0:T(512)(128)(4,1)S(1)} %compare_and_fusion.4, bf16[16,64,32]{1,2,0:T(8,128)(2,1)S(1)} %fusion.68), kind=kOutput, calls=%fused_computation.70 | convolution fusion | flops 69730304 | bytes 5308928 | tf_op jit(solution)/shard_map/jkr,jrd->jkd/dot_general | solution.py:40
  161.7 17.3 %all-to-all-done.1 = bf16[16,64,512]{2,1,0:T(8,128)(2,1)} async-done(((bf16[16,64,512]{2,1,0:T(8,128)(2,1)}), bf16[16,64,512]{2,1,0:T(8,128)(2,1)}, u32[]{:S(2)}, u32[]{:S(2)}) %all-to-all-start.1) | async-done | bytes 1048608 | tf_op jit(solution)/shard_map/all_to_all | solution.py:159
  179.0 4.9 %all-to-all-start.2 = ((bf16[16,64,2048]{2,1,0:T(8,128)(2,1)}), bf16[16,64,2048]{2,1,0:T(8,128)(2,1)}, u32[]{:S(2)}, u32[]{:S(2)}) async-start(bf16[16,64,2048]{2,1,0:T(8,128)(2,1)} %convolution_convert_fusion), calls=%async_computation.2 | async-start | bytes 8388608 | tf_op jit(solution)/shard_map/all_to_all | solution.py:158
  184.8 2.9 fusion.563
  189.2 3.3 gather_fusion.3
  192.5 3.6 fusion.3
  204.7 71.7 %all-to-all-done.2 = bf16[16,64,2048]{2,1,0:T(8,128)(2,1)} async-done(((bf16[16,64,2048]{2,1,0:T(8,128)(2,1)}), bf16[16,64,2048]{2,1,0:T(8,128)(2,1)}, u32[]{:S(2)}, u32[]{:S(2)}) %all-to-all-start.2) | async-done | bytes 4194336 | tf_op jit(solution)/shard_map/all_to_all | solution.py:158
  276.4 8.0 %gather_fusion.5 = bf16[512,2048]{1,0:T(8,128)(2,1)} fusion(bf16[1024,2048]{1,0:T(8,128)(2,1)} %bitcast.19, s32[1024]{0:T(1024)S(1)} %pad_clamp_fusion), kind=kCustom, calls=%fused_computation.5 | custom fusion | bytes 4196352 | tf_op jit(solution)/shard_map/gather | solution.py:161
  284.4 9.7 %convert_add_fusion = f32[512,2048]{1,0:T(8,128)} fusion(bf16[512,2048]{1,0:T(8,128)(2,1)} %gather_fusion.5, bf16[512,2048]{1,0:T(8,128)(2,1)S(1)} %copy-done, bf16[2048,2048]{1,0:T(8,128)(2,1)} %param.11), kind=kOutput, calls=%fused_computation.68 | convolution fusion | flops 4297064448 | bytes 16777216 | tf_op jit(solution)/shard_map/dot_general | solution.py:163
  294.1 5.3 %copy.65 = f32[512,2048]{0,1:T(8,128)} copy(f32[512,2048]{1,0:T(8,128)} %convert_add_fusion) | data formatting | bytes 8388608 | tf_op jit(solution)/shard_map/add | solution.py:163
  299.4 2.9 add_convert_fusion
  332.7 2.1 copy.72
  340.5 2.1 copy.71
  348.3 2.1 copy.70
  355.2 2.9 pad_maximum_fusion.1
  (226 shorter events, 64.3 us)
Async XLA Ops:
  6.5 3.6 copy-start
  20.6 122.1 %all-to-all-start = ((bf16[16,64,2048]{2,1,0:T(8,128)(2,1)}), bf16[16,64,2048]{2,1,0:T(8,128)(2,1)}, u32[]{:S(2)}, u32[]{:S(2)}) async-start(bf16[16,64,2048]{2,1,0:T(8,128)(2,1)} %broadcast_select_fusion), calls=%async_computation | async-start | bytes 8388608 | tf_op jit(solution)/shard_map/all_to_all | solution.py:155
  27.2 101.7 %copy-start.33 = (s32[512]{0:T(512)S(1)}, s32[512]{0:T(512)}, u32[]{:S(2)}) copy-start(s32[512]{0:T(512)} %param.17) | copy-start | bytes 6148
  27.2 102.3 %copy-start.29 = (bf16[32,16,256]{2,1,0:T(8,128)(2,1)S(1)}, bf16[32,16,256]{2,1,0:T(8,128)(2,1)}, u32[]{:S(2)}) copy-start(bf16[32,16,256]{2,1,0:T(8,128)(2,1)} %param.16) | copy-start | bytes 786436
  27.2 111.3 %all-gather.4.cloned.1.call-start = ((), (), s32[]{:S(2)}) async-start(), calls=%async_computation.3 | async-start | bytes 6291456 | tf_op jit(solution)/shard_map/all_gather | solution.py:148
  27.9 126.1 %all-gather.6.cloned.1.call-start = ((), (), s32[]{:S(2)}) async-start(), calls=%async_computation.4 | async-start | bytes 3145728 | tf_op jit(solution)/shard_map/all_gather | solution.py:149
  148.3 30.8 %all-to-all-start.1 = ((bf16[16,64,512]{2,1,0:T(8,128)(2,1)}), bf16[16,64,512]{2,1,0:T(8,128)(2,1)}, u32[]{:S(2)}, u32[]{:S(2)}) async-start(bf16[16,64,512]{2,1,0:T(8,128)(2,1)} %convolution_convert_fusion.1), calls=%async_computation.1 | async-start | bytes 2097152 | tf_op jit(solution)/shard_map/all_to_all | solution.py:159
  179.0 97.4 %all-to-all-start.2 = ((bf16[16,64,2048]{2,1,0:T(8,128)(2,1)}), bf16[16,64,2048]{2,1,0:T(8,128)(2,1)}, u32[]{:S(2)}, u32[]{:S(2)}) async-start(bf16[16,64,2048]{2,1,0:T(8,128)(2,1)} %convolution_convert_fusion), calls=%async_computation.2 | async-start | bytes 8388608 | tf_op jit(solution)/shard_map/all_to_all | solution.py:158
  184.2 3.4 copy-start.34
  331.1 3.7 %copy-start.24 = (f32[4,128,192]{1,2,0:T(8,128)S(1)}, f32[4,128,192]{1,2,0:T(8,128)}, u32[]{:S(2)}) copy-start(f32[4,128,192]{1,2,0:T(8,128)} %get-tuple-element.43) | copy-start | bytes 1179652
  331.4 4.5 %copy-start.23 = (f32[4,128,192]{1,2,0:T(8,128)S(1)}, f32[4,128,192]{1,2,0:T(8,128)}, u32[]{:S(2)}) copy-start(f32[4,128,192]{1,2,0:T(8,128)} %get-tuple-element.45) | copy-start | bytes 1179652
  331.7 5.3 %copy-start.22 = (f32[4,128,192]{1,2,0:T(8,128)S(1)}, f32[4,128,192]{1,2,0:T(8,128)}, u32[]{:S(2)}) copy-start(f32[4,128,192]{1,2,0:T(8,128)} %get-tuple-element.47) | copy-start | bytes 1179652
  332.7 5.4 %copy-start.21 = (f32[4,128,192]{1,2,0:T(8,128)S(1)}, f32[4,128,192]{1,2,0:T(8,128)}, u32[]{:S(2)}) copy-start(f32[4,128,192]{1,2,0:T(8,128)} %get-tuple-element.49) | copy-start | bytes 1179652
  334.8 3.4 copy-start.31
  334.9 3.6 copy-start.20
  338.9 3.8 %copy-start.16 = (f32[4,128,192]{1,2,0:T(8,128)S(1)}, f32[4,128,192]{1,2,0:T(8,128)}, u32[]{:S(2)}) copy-start(f32[4,128,192]{1,2,0:T(8,128)} %get-tuple-element.59) | copy-start | bytes 1179652
  339.2 4.5 %copy-start.15 = (f32[4,128,192]{1,2,0:T(8,128)S(1)}, f32[4,128,192]{1,2,0:T(8,128)}, u32[]{:S(2)}) copy-start(f32[4,128,192]{1,2,0:T(8,128)} %get-tuple-element.61) | copy-start | bytes 1179652
  339.5 5.3 %copy-start.14 = (f32[4,128,192]{1,2,0:T(8,128)S(1)}, f32[4,128,192]{1,2,0:T(8,128)}, u32[]{:S(2)}) copy-start(f32[4,128,192]{1,2,0:T(8,128)} %get-tuple-element.63) | copy-start | bytes 1179652
  340.5 5.4 %copy-start.13 = (f32[4,128,192]{1,2,0:T(8,128)S(1)}, f32[4,128,192]{1,2,0:T(8,128)}, u32[]{:S(2)}) copy-start(f32[4,128,192]{1,2,0:T(8,128)} %get-tuple-element.65) | copy-start | bytes 1179652
  342.6 3.4 copy-start.30
  342.7 3.6 copy-start.12
  346.7 3.8 %copy-start.8 = (f32[4,128,192]{1,2,0:T(8,128)S(1)}, f32[4,128,192]{1,2,0:T(8,128)}, u32[]{:S(2)}) copy-start(f32[4,128,192]{1,2,0:T(8,128)} %get-tuple-element.75) | copy-start | bytes 1179652
  347.0 3.7 %copy-start.7 = (f32[4,128,192]{1,2,0:T(8,128)S(1)}, f32[4,128,192]{1,2,0:T(8,128)}, u32[]{:S(2)}) copy-start(f32[4,128,192]{1,2,0:T(8,128)} %get-tuple-element.77) | copy-start | bytes 1179652
  353.8 4.3 %copy-start.1 = (bf16[512,2048]{1,0:T(8,128)(2,1)S(1)}, bf16[512,2048]{1,0:T(8,128)(2,1)}, u32[]{:S(2)}) copy-start(bf16[512,2048]{1,0:T(8,128)(2,1)} %param.10) | copy-start | bytes 6291460
  (19 other events, 27.0 us)
Sparse Core Ops, SparseCore 0:
  29.6 56.3 all-gather.3
  87.5 33.1 all-gather.5
where the time goes:
time: 366 us; the launch traced here: 365 us
  blocking collectives  109 us (30%)
  waiting for transfers between devices  90.5 us (25%)
  matrix products  64.4 us (18%)
  local copies, waits for them, and re-layouts  51.9 us (14%)
  other arithmetic  18 us (5%)
  starting transfers between devices  17.3 us (5%)
  between operations  14.3 us (4%)
    all_gather x1, blocking collectives, local(): lax.all_gather(adapter_per_request, 'store', axis=0, tiled=True)  100 us
    all_to_all x1, waiting for transfers between devices, local(): lax.all_to_all(query_update, 'store', split_axis=0, concat_axis=0, tiled=...  71.7 us
    dot_general x32, matrix products, attention(): jnp.einsum('qhd,kd->hqk', query_part, key_part, preferred_element_type=jn...  26.6 us
    all_to_all x1, waiting for transfers between devices, local(): lax.all_to_all(value_update, 'store', split_axis=0, concat_axis=0, tiled=...  17.3 us
    dot_general x32, matrix products, attention(): jnp.einsum('hqk,kd->qhd', weights, value_part, preferred_element_type=jnp...  11.5 us
    dot_general x1, matrix products, local(): jnp.dot(normalized_hidden_states, query_weight_matrix, preferred_element_...  9.7 us
    all_gather x1, blocking collectives, local(): lax.all_gather(adapter_up_value_weight, 'serve', axis=2, tiled=True)  8.38 us
    gather x1, local copies, waits for them, and re-layouts, local(): delta_query = query_update.reshape(-1, query_update.shape[2])[back_index]  7.95 us
  transfers between devices with their start and end apart: 5, of which 2 were waited for; matrix products, arithmetic and copies ran while one was open for 11% of the time, Pallas kernels for 0%

commit v1 on v0

v1 whole, which is shorter than its diff:
```python
import jax
import jax.numpy as jnp
from jax import lax
from jax.experimental import pallas as pl
from jax.experimental.pallas import tpu as pltpu
from jax.sharding import PartitionSpec as P

HEADS = 32
KV_HEADS = 8
HEAD_DIM = 64
RANK = 16
BLOCK = 64
LANES = 128
VMEM = pl.BlockSpec(memory_space=pltpu.VMEM)
CONTRACT_LAST = (((1,), (1,)), ((), ()))


def choose_kernel(pick_ref, down_ref, upq_ref, upv_ref, dsend_ref, qsend_ref, vsend_ref, sems):
    copies = []
    for dest in range(dsend_ref.shape[0]):
        entry = pick_ref[dest]
        copies.append(
            pltpu.make_async_copy(down_ref.at[entry], dsend_ref.at[dest], sems.at[0, dest])
        )
        copies.append(pltpu.make_async_copy(upq_ref.at[entry], qsend_ref.at[dest], sems.at[1, dest]))
        copies.append(pltpu.make_async_copy(upv_ref.at[entry], vsend_ref.at[dest], sems.at[2, dest]))
        for copy in copies[-3:]:
            copy.start()
    for copy in copies:
        copy.wait()


def choose(pick, down, upq, upv):
    count = pick.shape[0]
    anywhere = pl.BlockSpec(memory_space=pl.ANY)
    return pl.pallas_call(
        choose_kernel,
        out_shape=[
            jax.ShapeDtypeStruct((count,) + p.shape[1:], p.dtype) for p in (down, upq, upv)
        ],
        in_specs=[pl.BlockSpec(memory_space=pltpu.SMEM)] + [anywhere] * 3,
        out_specs=[anywhere] * 3,
        scratch_shapes=[pltpu.SemaphoreType.DMA((3, count))],
        name="choose",
    )(pick, down, upq, upv)


def low_kernel(x_ref, down_ref, owner_ref, lowq_ref, lowv_ref):
    serves, stores, _, _, width = down_ref.shape
    rows = x_ref.shape[0]
    cols = stores * RANK
    mine = owner_ref[:, :1] == lax.broadcasted_iota(jnp.int32, (rows, cols), 1) // RANK
    for part, out_ref in enumerate((lowq_ref, lowv_ref)):
        total = jnp.zeros((rows, cols), jnp.float32)
        for s in range(serves):
            total += lax.dot_general(
                x_ref[:, s * width : (s + 1) * width],
                down_ref[s, :, part].reshape(cols, width),
                CONTRACT_LAST,
                preferred_element_type=jnp.float32,
            )
        out_ref[...] = jnp.where(mine, total, 0.0).astype(jnp.bfloat16)


def low_products(x, down, owner):
    rows = x.shape[0]
    cols = down.shape[1] * RANK
    return pl.pallas_call(
        low_kernel,
        out_shape=[jax.ShapeDtypeStruct((rows, cols), jnp.bfloat16)] * 2,
        in_specs=[VMEM] * 3,
        out_specs=[VMEM] * 2,
        compiler_params=pltpu.CompilerParams(vmem_limit_bytes=32 << 20),
        name="low",
    )(x, down, owner)


def turned(x, cos, sin):
    lane = lax.broadcasted_iota(jnp.int32, x.shape, 1)
    other = jnp.where(
        lane % HEAD_DIM < HEAD_DIM // 2,
        pltpu.roll(x, LANES - HEAD_DIM // 2, 1),
        pltpu.roll(x, HEAD_DIM // 2, 1),
    )
    return x * cos + other * sin


def columns(ref):
    pieces, stores, rank, width = ref.shape
    parts = [ref[s].reshape(stores * rank, width) for s in range(pieces)]
    return parts[0] if pieces == 1 else jnp.concatenate(parts, axis=1)


def attend_kernel(
    baseq_ref, basek_ref, basev_ref, lowq_ref, lowv_ref, upq_ref, upv_ref, cos_ref, sin_ref, pos_ref, out_ref
):
    rows = baseq_ref.shape[0]
    half = lax.broadcasted_iota(jnp.int32, (rows, LANES), 1) < HEAD_DIM
    cos, sin = cos_ref[...], sin_ref[...]
    delta_q = jnp.dot(lowq_ref[...], columns(upq_ref), preferred_element_type=jnp.float32)
    base = baseq_ref[...] + delta_q.astype(jnp.bfloat16).astype(jnp.float32)
    query = [
        (turned(base[:, p * LANES : (p + 1) * LANES], cos, sin) * HEAD_DIM**-0.5).astype(jnp.bfloat16)
        for p in range(4)
    ]
    keys = turned(basek_ref[...], cos, sin)
    delta_v = jnp.dot(lowv_ref[...], columns(upv_ref), preferred_element_type=jnp.float32)
    values = basev_ref[...] + delta_v.astype(jnp.bfloat16).astype(jnp.float32)

    def split(x):
        left, right = jnp.where(half, x, 0.0), jnp.where(half, 0.0, x)
        return [
            (left.astype(jnp.bfloat16), pltpu.roll(left, HEAD_DIM, 1).astype(jnp.bfloat16)),
            (pltpu.roll(right, HEAD_DIM, 1).astype(jnp.bfloat16), right.astype(jnp.bfloat16)),
        ]

    key_parts, value_parts = split(keys), split(values)
    window = 2 * BLOCK
    ones_half = lax.broadcasted_iota(jnp.int32, (2 * window, LANES), 1) < HEAD_DIM
    ones_top = lax.broadcasted_iota(jnp.int32, (2 * window, LANES), 0) < window
    ones = jnp.where(ones_half == ones_top, 1.0, 0.0).astype(jnp.bfloat16)
    row = lax.broadcasted_iota(jnp.int32, (BLOCK, window), 0)
    col = lax.broadcasted_iota(jnp.int32, (BLOCK, window), 1)
    for b in range(rows // BLOCK):
        first = b * BLOCK
        start = max(0, first - BLOCK)
        here = slice(first, first + BLOCK)
        seen = slice(start, start + window)
        token, key = row + first, col + start
        allowed = (key <= token) & (key >= token - pos_ref[here, :])
        allowed = jnp.concatenate([allowed.astype(jnp.float32)] * 2, axis=0) > 0.5
        for g in range(2):
            kk = jnp.concatenate([part[seen] for part in key_parts[g]], axis=0)
            vv = jnp.concatenate([part[seen] for part in value_parts[g]], axis=0)
            vv = jnp.concatenate([vv, ones], axis=1)
            qq = jnp.concatenate([query[2 * g][here], query[2 * g + 1][here]], axis=0)
            scores = lax.dot_general(qq, kk, CONTRACT_LAST, preferred_element_type=jnp.float32)
            raised = []
            for side in range(2):
                s = jnp.where(allowed, scores[:, side * window : (side + 1) * window], -jnp.inf)
                raised.append(jnp.exp(s - jnp.max(s, axis=1, keepdims=True)))
            weights = jnp.concatenate(raised, axis=1).astype(jnp.bfloat16)
            mixed = jnp.dot(weights, vv, preferred_element_type=jnp.float32)
            done = (mixed[:, :LANES] / mixed[:, LANES:]).astype(jnp.bfloat16)
            for p in range(2):
                at = (2 * g + p) * LANES
                out_ref[here, at : at + LANES] = done[p * BLOCK : (p + 1) * BLOCK]


def up_spec(up, cols):
    serves, stores, rank, width = up.shape
    if width >= cols:
        per = width // cols
        return pl.BlockSpec((1, stores, rank, cols), lambda j: (j // per, 0, 0, j % per))
    return pl.BlockSpec((cols // width, stores, rank, width), lambda j: (j, 0, 0, 0))


def attend(baseq, basek, basev, lowq, lowv, upq, upv, cos, sin, pos):
    rows, width = baseq.shape
    steps = basek.shape[1] // LANES
    wide = width // steps

    def block(cols):
        return pl.BlockSpec((rows, cols), lambda j: (0, j))

    def whole(a):
        return pl.BlockSpec(a.shape, lambda j: (0, 0))

    return pl.pallas_call(
        attend_kernel,
        out_shape=jax.ShapeDtypeStruct((rows, width), jnp.bfloat16),
        grid=(steps,),
        in_specs=[
            block(wide),
            block(LANES),
            block(LANES),
            whole(lowq),
            whole(lowv),
            up_spec(upq, wide),
            up_spec(upv, LANES),
            whole(cos),
            whole(sin),
            whole(pos),
        ],
        out_specs=block(wide),
        compiler_params=pltpu.CompilerParams(vmem_limit_bytes=48 << 20),
        name="attend",
    )(baseq, basek, basev, lowq, lowv, upq, upv, cos, sin, pos)


def local(x, wq, wk, wv, down, upq, upv, panel_slot, adapters, lengths):
    axes = ("serve", "store")
    serves, stores = lax.axis_size("serve"), lax.axis_size("store")
    my_store = lax.axis_index("store")
    rows = x.shape[0]
    per_store = down.shape[0]
    lengths, adapters = lengths[0], adapters[0]
    requests = lengths.shape[0]

    entries = jnp.arange(panel_slot.shape[0], dtype=jnp.int32)
    slots = jnp.sum(jnp.where(adapters[:, None] == entries[None, :], panel_slot[None, :], 0), axis=1)
    owners = slots // per_store
    store_ids = jnp.arange(stores, dtype=jnp.int32)
    asked = jnp.sum(
        jnp.where(owners[None, :] == store_ids[:, None], slots[None, :] % per_store, 0), axis=1
    )
    all_asked = lax.all_gather(asked[None, :], axes, axis=0, tiled=True)
    pick = jnp.sum(jnp.where(store_ids[None, :] == my_store, all_asked, 0), axis=1)
    down_send, upq_send, upv_send = choose(pick, down, upq, upv)

    def exchange(a):
        return lax.all_to_all(a, axes, split_axis=0, concat_axis=0, tiled=True)

    width = down.shape[2]
    down_got = exchange(down_send).reshape(serves, stores, 2, RANK, width)
    upq_got = exchange(upq_send).reshape(serves, stores, RANK, width)
    upv_got = exchange(upv_send).reshape(serves, stores, RANK, upv.shape[2])

    order = jnp.arange(requests, dtype=jnp.int32)
    ends = jnp.sum(jnp.where(order[None, :] <= order[:, None], lengths[None, :], 0), axis=1)
    token = jnp.arange(rows, dtype=jnp.int32)
    member = (token[:, None] < ends[None, :]) & (token[:, None] >= (ends - lengths)[None, :])
    positions = token - jnp.sum(jnp.where(member, (ends - lengths)[None, :], 0), axis=1)
    owner = jnp.sum(jnp.where(member, owners[None, :], 0), axis=1)
    frequency = 500000.0 ** (
        -(jnp.arange(HEAD_DIM // 2).astype(jnp.float32) * 2.0 / HEAD_DIM)
    )
    angles = positions.astype(jnp.float32)[:, None] * frequency[None, :]
    cos, sin = jnp.cos(angles), jnp.sin(angles)
    cos = jnp.concatenate([cos] * 4, axis=1)
    sin = jnp.concatenate([-sin, sin] * 2, axis=1)
    pos = jnp.broadcast_to(positions[:, None], (rows, LANES))
    owner = jnp.broadcast_to(owner[:, None], (rows, LANES))

    baseq = jnp.dot(x, wq, preferred_element_type=jnp.float32)
    basek = jnp.dot(x, wk, preferred_element_type=jnp.float32)
    basev = jnp.dot(x, wv, preferred_element_type=jnp.float32)
    lowq, lowv = low_products(x, down_got, owner)
    return attend(baseq, basek, basev, lowq, lowv, upq_got, upv_got, cos, sin, pos)


def solution(mesh):
    both = P(("serve", "store"), None)
    panel = P("store", None, "serve")
    return jax.shard_map(
        local,
        mesh=mesh,
        in_specs=(both, P(), P(), P(), panel, panel, panel, P(), both, both),
        out_specs=both,
        check_vma=False,
    )
```

time: 366 us -> 271 us (0.74); the launches traced: 365 us -> 266 us
  Pallas kernels: 0 us -> 124 us
  blocking collectives: 109 us -> 53.2 us
  matrix products: 64.4 us -> 15.6 us
  waiting for transfers between devices: 90.5 us -> 44.5 us
  local copies, waits for them, and re-layouts: 51.9 us -> 8.21 us
  between operations: 14.3 us -> 0.12 us
  other arithmetic: 18 us -> 6.73 us
  starting transfers between devices: 17.3 us -> 13.4 us
    pallas_call x0 -> x3, Pallas kernels: none -> 124 us  [the longest x1 106 us: choose(): pl.pallas_call(choose_kernel, out_shape=[jax.ShapeDtypeStruct((count,) +...]
    all_gather x2 -> x0, blocking collectives: 109 us -> none  [the longest x1 100 us: local(): lax.all_gather(adapter_per_request, 'store', axis=0, tiled=True)]
    dot_general x70 -> x3, matrix products: 64.4 us -> 15.6 us  [the longest x1 9.36 us: local(): baseq = jnp.dot(x, wq, preferred_element_type=jnp.float32)]
    all_to_all x3 -> x2, waiting for transfers between devices: 89.1 us -> 44.5 us  [exchange(): return lax.all_to_all(a, axes, split_axis=0, concat_axis=0, tiled=True)]
    unnamed x0 -> x1, blocking collectives: none -> 39.5 us
    gather x6 -> x0, local copies, waits for them, and re-layouts: 25.2 us -> none  [the longest x1 7.95 us: local(): delta_query = query_update.reshape(-1, query_update.shape[2])[back_index]]
    all_to_all x0 -> x1, blocking collectives: none -> 13.7 us  [exchange(): return lax.all_to_all(a, axes, split_axis=0, concat_axis=0, tiled=True)]
    convert_element_type x5 -> x0, local copies, waits for them, and re-layouts: 8.96 us -> none  [the longest x4 7.71 us: attention(): outputs.append(jnp.concatenate(pieces, axis=1).reshape(block_rows, HEADS...]
  transfers between devices with their start and end apart: 5 -> 2, of which waited for: 2 -> 2; matrix products, arithmetic and copies ran while one was open for 11% -> 8% of each run, Pallas kernels for 0% -> 1%
where the time goes in v1:
time: 271 us; the launch traced here: 266 us
  Pallas kernels  124 us (46%)
  blocking collectives  53.2 us (20%)
  waiting for transfers between devices  44.5 us (16%)
  matrix products  15.6 us (6%)
  starting transfers between devices  13.4 us (5%)
  local copies, waits for them, and re-layouts  8.21 us (3%)
  other arithmetic  6.73 us (2%)
    pallas_call x1, Pallas kernels, choose(): pl.pallas_call(choose_kernel, out_shape=[jax.ShapeDtypeStruct((count,) +...  106 us
    all_to_all x2, waiting for transfers between devices, exchange(): return lax.all_to_all(a, axes, split_axis=0, concat_axis=0, tiled=True)  44.5 us
    unnamed x1, blocking collectives  39.5 us
    pallas_call x1, Pallas kernels, attend(): pl.pallas_call(attend_kernel, out_shape=jax.ShapeDtypeStruct((rows, width...  15.3 us
    all_to_all x1, blocking collectives, exchange(): return lax.all_to_all(a, axes, split_axis=0, concat_axis=0, tiled=True)  13.7 us
    all_to_all x2, starting transfers between devices, exchange(): return lax.all_to_all(a, axes, split_axis=0, concat_axis=0, tiled=True)  13.4 us
    dot_general x1, matrix products, local(): baseq = jnp.dot(x, wq, preferred_element_type=jnp.float32)  9.36 us
    unnamed x26, local copies, waits for them, and re-layouts  7.9 us
  transfers between devices with their start and end apart: 2, of which 2 were waited for; matrix products, arithmetic and copies ran while one was open for 8% of the time, Pallas kernels for 1%

profile of v1, /device:TPU:15, one launch (start us, length us, event | category | flops | bytes accessed | tf_op | source)
XLA Modules:
  0.0 265.8 jit_solution(10875576745663410324)
XLA Ops:
  0.0 1.0 select_reduce_fusion.2
  1.4 39.5 %all-reduce = s32[512]{0:T(512)S(1)} all-reduce(s32[512]{0:T(512)S(1)} %dynamic-update-slice), channel_id=2, replica_groups=mesh['serve'=2,'store'=16] {'serve','store'}, use_global_device_ids=true, to_apply=%add | all-reduce | flops 512 | bytes 4096
  41.0 0.7 select_reduce_fusion.3.pick_ref
  41.7 105.9 %choose.1 = (bf16[32,32,1024]{2,1,0:T(8,128)(2,1)}, bf16[32,16,1024]{2,1,0:T(8,128)(2,1)}, bf16[32,16,256]{2,1,0:T(8,128)(2,1)}) custom-call(s32[32]{0:T(128)} %select_reduce_fusion.3.pick_ref, bf16[32,32,1024]{2,1,0:T(8,128)(2,1)} %down_ref.1, bf16[32,16,1024]{2,1,0:T(8,128)(2,1)} %upq_ref.1, bf16[32,16,256]{2,1,0:T(8,128)(2,1)} %upv_ref.1), custom_call_target="tpu_custom_call" | custom-call | tf_op jit(solution)/shard_map/choose/pallas_call | solution.py:36
  147.6 13.7 %all_to_all.15 = bf16[32,16,256]{2,1,0:T(8,128)(2,1)} all-to-all(bf16[32,16,256]{2,1,0:T(8,128)(2,1)} %get-tuple-element.14), channel_id=1, replica_groups=mesh['serve'=2,'store'=16] {'serve','store'}, dimensions={0} | all-to-all | bytes 524288 | tf_op jit(solution)/shard_map/all_to_all | solution.py:212
  161.2 6.1 %all-to-all-start = ((bf16[32,32,1024]{2,1,0:T(8,128)(2,1)}), bf16[32,32,1024]{2,1,0:T(8,128)(2,1)}, u32[]{:S(2)}, u32[]{:S(2)}) async-start(bf16[32,32,1024]{2,1,0:T(8,128)(2,1)} %get-tuple-element.10), calls=%async_computation | async-start | bytes 4194304 | tf_op jit(solution)/shard_map/all_to_all | solution.py:212
  167.6 1.9 fusion
  169.5 43.4 %all-to-all-done = bf16[32,32,1024]{2,1,0:T(8,128)(2,1)} async-done(((bf16[32,32,1024]{2,1,0:T(8,128)(2,1)}), bf16[32,32,1024]{2,1,0:T(8,128)(2,1)}, u32[]{:S(2)}, u32[]{:S(2)}) %all-to-all-start) | async-done | bytes 2097184 | tf_op jit(solution)/shard_map/all_to_all | solution.py:212
  212.9 7.3 %all-to-all-start.1 = ((bf16[32,16,1024]{2,1,0:T(8,128)(2,1)}), bf16[32,16,1024]{2,1,0:T(8,128)(2,1)S(1)}, u32[]{:S(2)}, u32[]{:S(2)}) async-start(bf16[32,16,1024]{2,1,0:T(8,128)(2,1)} %get-tuple-element.13), calls=%async_computation.1 | async-start | bytes 2097152 | tf_op jit(solution)/shard_map/all_to_all | solution.py:212
  220.2 2.8 %pad_maximum_fusion = (f32[512,128]{1,0:T(8,128)S(1)}, f32[512,128]{1,0:T(8,128)}) fusion(f32[512,32]{1,0:T(8,128)} %get-tuple-element.19, f32[512,32]{1,0:T(8,128)} %get-tuple-element.18, f32[512,32]{1,0:T(8,128)} %get-tuple-element.17), kind=kLoop, calls=%fused_computation.2 | loop fusion | flops 393216 | bytes 720896 | tf_op jit(solution)/shard_map/concatenate | solution.py:230
  223.0 4.0 %fusion.5.basek_ref = f32[512,512]{1,0:T(8,128)} fusion(bf16[512,2048]{1,0:T(8,128)(2,1)} %x_ref.1, bf16[2048,512]{1,0:T(8,128)(2,1)S(1)} %copy-done), kind=kOutput, calls=%fused_computation.29 | convolution fusion | flops 1073741824 | bytes 5242880 | tf_op jit(solution)/shard_map/dot_general | solution.py:236
  227.0 2.2 fusion.6.basev_ref
  229.2 9.4 %fusion.4.baseq_ref = f32[512,2048]{1,0:T(8,128)} fusion(bf16[512,2048]{1,0:T(8,128)(2,1)S(1)} %copy-done.1, bf16[2048,2048]{1,0:T(8,128)(2,1)} %param.11), kind=kOutput, calls=%fused_computation.28 | convolution fusion | flops 4294967296 | bytes 14680064 | tf_op jit(solution)/shard_map/dot_general | solution.py:235
  238.7 2.9 %low.1 = (bf16[512,256]{1,0:T(8,128)(2,1)S(1)}, bf16[512,256]{1,0:T(8,128)(2,1)S(1)}) custom-call(bf16[512,2048]{1,0:T(8,128)(2,1)S(1)} %copy-done.1, bf16[2,16,2,16,1024]{4,3,2,1,0:T(8,128)(2,1)} %bitcast.1.down_ref, s32[512,128]{1,0:T(8,128)S(1)} %broadcast_in_dim.102.owner_ref), custom_call_target="tpu_custom_call" | custom-call | tf_op jit(solution)/shard_map/low/pallas_call | solution.py:68
  241.6 0.7 copy-done.6
  242.3 0.7 copy-done.8
  243.0 1.0 all-to-all-done.1
  244.2 0.9 copy-done.2
  245.1 0.9 copy-done.3
  246.1 1.2 copy-done.4
  247.3 1.2 copy-done.5
  248.5 0.9 copy-done.7
  249.5 0.9 copy-done.9
  250.4 15.3 %attend.1 = bf16[512,2048]{1,0:T(8,128)(2,1)} custom-call(f32[512,2048]{1,0:T(8,128)} %fusion.4.baseq_ref, f32[512,512]{1,0:T(8,128)S(1)} %copy-done.4, f32[512,512]{1,0:T(8,128)S(1)} %copy-done.5, bf16[512,256]{1,0:T(8,128)(2,1)S(1)} %copy-done.7, bf16[512,256]{1,0:T(8,128)(2,1)S(1)} %copy-done.9, bf16[2,16,16,1024]{3,2,1,0:T(8,128)(2,1)S(1)} %bitcast.17, ...), custom_call_target="tpu_custom_call" | custom-call | tf_op jit(solution)/shard_map/attend/pallas_call | solution.py:169
  (29 shorter events, 1.0 us)
Async XLA Ops:
  0.0 223.0 %copy-start = (bf16[2048,512]{1,0:T(8,128)(2,1)S(1)}, bf16[2048,512]{1,0:T(8,128)(2,1)}, u32[]{:S(2)}) copy-start(bf16[2048,512]{1,0:T(8,128)(2,1)} %param.12) | copy-start | bytes 6291460
  161.2 6.1 %copy-start.11 = (s32[1,16]{1,0:T(1,128)S(1)}, s32[1,16]{1,0:T(1,128)}, u32[]{:S(2)}) copy-start(s32[1,16]{1,0:T(1,128)} %param.19) | copy-start | bytes 196
  161.2 51.7 %all-to-all-start = ((bf16[32,32,1024]{2,1,0:T(8,128)(2,1)}), bf16[32,32,1024]{2,1,0:T(8,128)(2,1)}, u32[]{:S(2)}, u32[]{:S(2)}) async-start(bf16[32,32,1024]{2,1,0:T(8,128)(2,1)} %get-tuple-element.10), calls=%async_computation | async-start | bytes 4194304 | tf_op jit(solution)/shard_map/all_to_all | solution.py:212
  212.9 31.1 %all-to-all-start.1 = ((bf16[32,16,1024]{2,1,0:T(8,128)(2,1)}), bf16[32,16,1024]{2,1,0:T(8,128)(2,1)S(1)}, u32[]{:S(2)}, u32[]{:S(2)}) async-start(bf16[32,16,1024]{2,1,0:T(8,128)(2,1)} %get-tuple-element.13), calls=%async_computation.1 | async-start | bytes 2097152 | tf_op jit(solution)/shard_map/all_to_all | solution.py:212
  223.0 4.0 %copy-start.1 = (bf16[512,2048]{1,0:T(8,128)(2,1)S(1)}, bf16[512,2048]{1,0:T(8,128)(2,1)}, u32[]{:S(2)}) copy-start(bf16[512,2048]{1,0:T(8,128)(2,1)} %x_ref.1) | copy-start | bytes 6291460
  223.0 4.0 %copy-start.10 = (bf16[2048,512]{1,0:T(8,128)(2,1)S(1)}, bf16[2048,512]{1,0:T(8,128)(2,1)}, u32[]{:S(2)}) copy-start(bf16[2048,512]{1,0:T(8,128)(2,1)} %param.13) | copy-start | bytes 6291460
  241.6 0.7 copy-start.6
  242.3 0.7 copy-start.8
  244.2 1.0 copy-start.2
  245.1 0.9 copy-start.3
  246.1 1.2 copy-start.4
  247.3 1.2 copy-start.5
  248.5 0.9 copy-start.7
  249.5 0.9 copy-start.9

commit v2 on v1

--- a/solution.py
+++ b/solution.py
@@ -1,3 +1,5 @@
+import functools
+
 import jax
 import jax.numpy as jnp
 from jax import lax
@@ -15,32 +17,99 @@
 CONTRACT_LAST = (((1,), (1,)), ((), ()))
 
 
-def choose_kernel(pick_ref, down_ref, upq_ref, upv_ref, dsend_ref, qsend_ref, vsend_ref, sems):
-    copies = []
-    for dest in range(dsend_ref.shape[0]):
+def ask_kernel(serves, stores, asked_ref, all_ref, send_sems, recv_sems):
+    count = serves * stores
+    me = lax.axis_index("serve") * stores + lax.axis_index("store")
+
+    def peer(step):
+        there = lax.rem(me + step, count)
+        return (there // stores, lax.rem(there, stores))
+
+    def copy(step):
+        return pltpu.make_async_remote_copy(
+            src_ref=asked_ref,
+            dst_ref=all_ref.at[me],
+            send_sem=send_sems.at[step],
+            recv_sem=recv_sems.at[step],
+            device_id=peer(step),
+            device_id_type=pl.DeviceIdType.MESH,
+        )
+
+    barrier = pltpu.get_barrier_semaphore()
+
+    @pl.loop(1, count)
+    def _(step):
+        pl.semaphore_signal(
+            barrier, inc=1, device_id=peer(step), device_id_type=pl.DeviceIdType.MESH
+        )
+
+    pl.semaphore_wait(barrier, count - 1)
+
+    @pl.loop(1, count)
+    def _(step):
+        copy(step).start()
+
+    all_ref[me] = asked_ref[...]
+
+    @pl.loop(1, count)
+    def _(step):
+        copy(step).wait()
+
+
+def ask(asked, serves, stores):
+    count = serves * stores
+    return pl.pallas_call(
+        functools.partial(ask_kernel, serves, stores),
+        out_shape=jax.ShapeDtypeStruct((count,) + asked.shape, asked.dtype),
+        in_specs=[VMEM],
+        out_specs=VMEM,
+        scratch_shapes=[pltpu.SemaphoreType.DMA((count,)), pltpu.SemaphoreType.DMA((count,))],
+        compiler_params=pltpu.CompilerParams(collective_id=0, has_side_effects=True),
+        name="ask",
+    )(asked)
+
+
+def choose_kernel(joined, pick_ref, down_ref, upq_ref, upv_ref, dsend_ref, *rest):
+    qsend_ref, vsend_ref, sems = (rest[0], rest[0], rest[1]) if joined else rest
+    width = upq_ref.shape[2]
+
+    def copies(dest):
         entry = pick_ref[dest]
-        copies.append(
-            pltpu.make_async_copy(down_ref.at[entry], dsend_ref.at[dest], sems.at[0, dest])
+        if joined:
+            q_to = qsend_ref.at[dest, :, pl.ds(0, width)]
+            v_to = vsend_ref.at[dest, :, pl.ds(width, upv_ref.shape[2])]
+        else:
+            q_to, v_to = qsend_ref.at[dest], vsend_ref.at[dest]
+        return (
+            pltpu.make_async_copy(down_ref.at[entry], dsend_ref.at[dest], sems.at[0, dest]),
+            pltpu.make_async_copy(upq_ref.at[entry], q_to, sems.at[1, dest]),
+            pltpu.make_async_copy(upv_ref.at[entry], v_to, sems.at[2, dest]),
         )
-        copies.append(pltpu.make_async_copy(upq_ref.at[entry], qsend_ref.at[dest], sems.at[1, dest]))
-        copies.append(pltpu.make_async_copy(upv_ref.at[entry], vsend_ref.at[dest], sems.at[2, dest]))
-        for copy in copies[-3:]:
+
+    @pl.loop(0, dsend_ref.shape[0])
+    def _(dest):
+        for copy in copies(dest):
             copy.start()
-    for copy in copies:
-        copy.wait()
-
-
-def choose(pick, down, upq, upv):
+
+    @pl.loop(0, dsend_ref.shape[0])
+    def _(dest):
+        for copy in copies(dest):
+            copy.wait()
+
+
+def choose(pick, down, upq, upv, joined):
     count = pick.shape[0]
     anywhere = pl.BlockSpec(memory_space=pl.ANY)
+    shapes = [down.shape[1:], upq.shape[1:], upv.shape[1:]]
+    if joined:
+        shapes[1:] = [(upq.shape[1], upq.shape[2] + upv.shape[2])]
     return pl.pallas_call(
-        choose_kernel,
-        out_shape=[
-            jax.ShapeDtypeStruct((count,) + p.shape[1:], p.dtype) for p in (down, upq, upv)
-        ],
+        functools.partial(choose_kernel, joined),
+        out_shape=[jax.ShapeDtypeStruct((count,) + shape, down.dtype) for shape in shapes],
         in_specs=[pl.BlockSpec(memory_space=pltpu.SMEM)] + [anywhere] * 3,
-        out_specs=[anywhere] * 3,
+        out_specs=[VMEM] * len(shapes),
         scratch_shapes=[pltpu.SemaphoreType.DMA((3, count))],
+        compiler_params=pltpu.CompilerParams(vmem_limit_bytes=32 << 20),
         name="choose",
     )(pick, down, upq, upv)
 
@@ -147,15 +216,15 @@
                 out_ref[here, at : at + LANES] = done[p * BLOCK : (p + 1) * BLOCK]
 
 
-def up_spec(up, cols):
-    serves, stores, rank, width = up.shape
+def up_spec(up, width, skip, cols):
+    _, stores, rank, _ = up.shape
     if width >= cols:
-        per = width // cols
-        return pl.BlockSpec((1, stores, rank, cols), lambda j: (j // per, 0, 0, j % per))
+        per, off = width // cols, skip // cols
+        return pl.BlockSpec((1, stores, rank, cols), lambda j: (j // per, 0, 0, off + j % per))
     return pl.BlockSpec((cols // width, stores, rank, width), lambda j: (j, 0, 0, 0))
 
 
-def attend(baseq, basek, basev, lowq, lowv, upq, upv, cos, sin, pos):
+def attend(baseq, basek, basev, lowq, lowv, upq, upv, cos, sin, pos, serves, joined):
     rows, width = baseq.shape
     steps = basek.shape[1] // LANES
     wide = width // steps
@@ -176,8 +245,8 @@
             block(LANES),
             whole(lowq),
             whole(lowv),
-            up_spec(upq, wide),
-            up_spec(upv, LANES),
+            up_spec(upq, width // serves, 0, wide),
+            up_spec(upv, basev.shape[1] // serves, width // serves if joined else 0, LANES),
             whole(cos),
             whole(sin),
             whole(pos),
@@ -204,17 +273,19 @@
     asked = jnp.sum(
         jnp.where(owners[None, :] == store_ids[:, None], slots[None, :] % per_store, 0), axis=1
     )
-    all_asked = lax.all_gather(asked[None, :], axes, axis=0, tiled=True)
-    pick = jnp.sum(jnp.where(store_ids[None, :] == my_store, all_asked, 0), axis=1)
-    down_send, upq_send, upv_send = choose(pick, down, upq, upv)
+    row = jnp.pad(asked, (0, LANES - stores))[None, :]
+    all_asked = ask(row, serves, stores)[:, 0, :]
+    lanes = jnp.arange(LANES, dtype=jnp.int32)
+    pick = jnp.sum(jnp.where(lanes[None, :] == my_store, all_asked, 0), axis=1)
+    joined = upv.shape[2] % LANES == 0
 
     def exchange(a):
         return lax.all_to_all(a, axes, split_axis=0, concat_axis=0, tiled=True)
 
-    width = down.shape[2]
-    down_got = exchange(down_send).reshape(serves, stores, 2, RANK, width)
-    upq_got = exchange(upq_send).reshape(serves, stores, RANK, width)
-    upv_got = exchange(upv_send).reshape(serves, stores, RANK, upv.shape[2])
+    down_got, *up_got = [exchange(a) for a in choose(pick, down, upq, upv, joined)]
+    down_got = down_got.reshape(serves, stores, 2, RANK, down.shape[2])
+    up_got = [a.reshape((serves, stores) + a.shape[1:]) for a in up_got]
+    upq_got, upv_got = up_got[0], up_got[-1]
 
     order = jnp.arange(requests, dtype=jnp.int32)
     ends = jnp.sum(jnp.where(order[None, :] <= order[:, None], lengths[None, :], 0), axis=1)
@@ -236,7 +307,7 @@
     basek = jnp.dot(x, wk, preferred_element_type=jnp.float32)
     basev = jnp.dot(x, wv, preferred_element_type=jnp.float32)
     lowq, lowv = low_products(x, down_got, owner)
-    return attend(baseq, basek, basev, lowq, lowv, upq_got, upv_got, cos, sin, pos)
+    return attend(baseq, basek, basev, lowq, lowv, upq_got, upv_got, cos, sin, pos, serves, joined)
 
 
 def solution(mesh):

time: 271 us -> 139 us (0.51)
  the two profiles are of different devices: /device:TPU:15 before, /device:TPU:0 now
where the time goes in v2:
time: 139 us; the launch traced here: 138 us
  waiting for transfers between devices  65.2 us (47%)
  Pallas kernels  35.2 us (25%)
  local copies, waits for them, and re-layouts  14.6 us (11%)
  matrix products  10.6 us (8%)
  starting transfers between devices  7.97 us (6%)
  other arithmetic  4.54 us (3%)
    all_to_all x2, waiting for transfers between devices, exchange(): return lax.all_to_all(a, axes, split_axis=0, concat_axis=0, tiled=True)  65.2 us
    pallas_call x1, Pallas kernels, attend(): pl.pallas_call(attend_kernel, out_shape=jax.ShapeDtypeStruct((rows, width...  15.4 us
    unnamed x36, local copies, waits for them, and re-layouts  13.8 us
    pallas_call x1, Pallas kernels, ask(): pl.pallas_call(functools.partial(ask_kernel, serves, stores), out_shape=j...  11.3 us
    all_to_all x2, starting transfers between devices, exchange(): return lax.all_to_all(a, axes, split_axis=0, concat_axis=0, tiled=True)  7.97 us
    dot_general x1, matrix products, local(): baseq = jnp.dot(x, wq, preferred_element_type=jnp.float32)  6.03 us
    pallas_call x1, Pallas kernels, choose(): pl.pallas_call(functools.partial(choose_kernel, joined), out_shape=[jax.S...  5.55 us
    pallas_call x1, Pallas kernels, low_products(): pl.pallas_call(low_kernel, out_shape=[jax.ShapeDtypeStruct((rows, cols),...  2.88 us
  transfers between devices with their start and end apart: 2, of which 2 were waited for; matrix products, arithmetic and copies ran while one was open for 10% of the time, Pallas kernels for 2%

profile of v2, /device:TPU:0, one launch (start us, length us, event | category | flops | bytes accessed | tf_op | source)
XLA Modules:
  0.0 138.2 jit_solution(10175979095729063437)
XLA Ops:
  0.0 1.0 select_reduce_fusion.2
  1.7 11.3 %ask.1 = s32[32,1,128]{2,1,0:T(1,128)} custom-call(s32[1,128]{1,0:T(1,128)} %pad_bitcast_fusion.asked_ref), custom_call_target="tpu_custom_call" | custom-call | tf_op jit(solution)/shard_map/ask/pallas_call | solution.py:61
  13.8 1.6 %copy-done.1 = bf16[32,32,1024]{2,1,0:T(8,128)(2,1)S(1)} copy-done((bf16[32,32,1024]{2,1,0:T(8,128)(2,1)S(1)}, bf16[32,32,1024]{2,1,0:T(8,128)(2,1)}, u32[]{:S(2)}) %copy-start.1) | copy-done | bytes 2097176
  15.4 1.2 copy-done.9
  16.6 0.9 copy-done.10
  17.6 5.6 %choose.1 = (bf16[32,32,1024]{2,1,0:T(8,128)(2,1)S(1)}, bf16[32,16,1280]{2,1,0:T(8,128)(2,1)S(1)}) custom-call(s32[32]{0:T(128)S(1)} %select_reduce_fusion.3.pick_ref, bf16[32,32,1024]{2,1,0:T(8,128)(2,1)S(1)} %copy-done.1, bf16[32,16,1024]{2,1,0:T(8,128)(2,1)S(1)} %copy-done.9, bf16[32,16,256]{2,1,0:T(8,128)(2,1)S(1)} %copy-done.10), custom_call_target="tpu_custom_call" | custom-call | tf_op jit(solution)/shard_map/choose/pallas_call | solution.py:106
  23.2 1.3 copy-done.3
  24.5 1.1 copy-done.4
  25.6 5.3 %all-to-all-start = ((bf16[32,32,1024]{2,1,0:T(8,128)(2,1)}), bf16[32,32,1024]{2,1,0:T(8,128)(2,1)}, u32[]{:S(2)}, u32[]{:S(2)}) async-start(bf16[32,32,1024]{2,1,0:T(8,128)(2,1)} %copy-done.3), calls=%async_computation | async-start | bytes 4194304 | tf_op jit(solution)/shard_map/all_to_all | solution.py:283
  31.1 49.8 %all-to-all-done = bf16[32,32,1024]{2,1,0:T(8,128)(2,1)} async-done(((bf16[32,32,1024]{2,1,0:T(8,128)(2,1)}), bf16[32,32,1024]{2,1,0:T(8,128)(2,1)}, u32[]{:S(2)}, u32[]{:S(2)}) %all-to-all-start) | async-done | bytes 2097184 | tf_op jit(solution)/shard_map/all_to_all | solution.py:283
  80.9 2.7 %all-to-all-start.1 = ((bf16[32,16,1280]{2,1,0:T(8,128)(2,1)}), bf16[32,16,1280]{2,1,0:T(8,128)(2,1)S(1)}, u32[]{:S(2)}, u32[]{:S(2)}) async-start(bf16[32,16,1280]{2,1,0:T(8,128)(2,1)} %copy-done.4), calls=%async_computation.1 | async-start | bytes 2621440 | tf_op jit(solution)/shard_map/all_to_all | solution.py:283
  83.6 1.0 fusion
  84.6 1.3 pad_maximum_fusion
  86.0 2.2 %fusion.5.basek_ref = f32[512,512]{1,0:T(8,128)} fusion(bf16[512,2048]{1,0:T(8,128)(2,1)S(1)} %copy-done.2, bf16[2048,512]{1,0:T(8,128)(2,1)S(1)} %copy-done), kind=kOutput, calls=%fused_computation.30 | convolution fusion | flops 1073741824 | bytes 5242880 | tf_op jit(solution)/shard_map/dot_general | solution.py:307
  88.2 2.3 %fusion.6.basev_ref = f32[512,512]{1,0:T(8,128)} fusion(bf16[512,2048]{1,0:T(8,128)(2,1)S(1)} %copy-done.2, bf16[2048,512]{1,0:T(8,128)(2,1)S(1)} %copy-done.16), kind=kOutput, calls=%fused_computation.31 | convolution fusion | flops 1073741824 | bytes 5242880 | tf_op jit(solution)/shard_map/dot_general | solution.py:308
  90.5 6.0 %fusion.4.baseq_ref = f32[512,2048]{1,0:T(8,128)} fusion(bf16[512,2048]{1,0:T(8,128)(2,1)S(1)} %copy-done.2, bf16[2048,2048]{1,0:T(8,128)(2,1)S(1)} %copy-done.15), kind=kOutput, calls=%fused_computation.29 | convolution fusion | flops 4294967296 | bytes 14680064 | tf_op jit(solution)/shard_map/dot_general | solution.py:306
  96.7 2.9 %low.1 = (bf16[512,256]{1,0:T(8,128)(2,1)S(1)}, bf16[512,256]{1,0:T(8,128)(2,1)S(1)}) custom-call(bf16[512,2048]{1,0:T(8,128)(2,1)S(1)} %copy-done.2, bf16[2,16,2,16,1024]{4,3,2,1,0:T(8,128)(2,1)} %bitcast.3.down_ref, s32[512,128]{1,0:T(8,128)S(1)} %broadcast_in_dim.102.owner_ref), custom_call_target="tpu_custom_call" | custom-call | tf_op jit(solution)/shard_map/low/pallas_call | solution.py:137
  101.0 15.4 %all-to-all-done.1 = bf16[32,16,1280]{2,1,0:T(8,128)(2,1)S(1)} async-done(((bf16[32,16,1280]{2,1,0:T(8,128)(2,1)}), bf16[32,16,1280]{2,1,0:T(8,128)(2,1)S(1)}, u32[]{:S(2)}, u32[]{:S(2)}) %all-to-all-start.1) | async-done | bytes 1310752 | tf_op jit(solution)/shard_map/all_to_all | solution.py:283
  116.5 1.2 copy-done.5
  117.7 1.2 copy-done.6
  118.9 0.9 copy-done.7
  119.9 0.9 copy-done.8
  120.8 0.9 copy-done.12
  122.7 15.4 %attend.1 = bf16[512,2048]{1,0:T(8,128)(2,1)} custom-call(f32[512,2048]{1,0:T(8,128)} %fusion.4.baseq_ref, f32[512,512]{1,0:T(8,128)S(1)} %copy-done.5, f32[512,512]{1,0:T(8,128)S(1)} %copy-done.6, bf16[512,256]{1,0:T(8,128)(2,1)S(1)} %copy-done.12, bf16[512,256]{1,0:T(8,128)(2,1)S(1)} %copy-done.14, bf16[2,16,16,1280]{3,2,1,0:T(8,128)(2,1)S(1)} %bitcast.19, ...), custom_call_target="tpu_custom_call" | custom-call | tf_op jit(solution)/shard_map/attend/pallas_call | solution.py:238
  (38 shorter events, 4.3 us)
Async XLA Ops:
  0.0 86.0 %copy-start = (bf16[2048,512]{1,0:T(8,128)(2,1)S(1)}, bf16[2048,512]{1,0:T(8,128)(2,1)}, u32[]{:S(2)}) copy-start(bf16[2048,512]{1,0:T(8,128)(2,1)} %param.12) | copy-start | bytes 6291460
  13.8 1.6 %copy-start.1 = (bf16[32,32,1024]{2,1,0:T(8,128)(2,1)S(1)}, bf16[32,32,1024]{2,1,0:T(8,128)(2,1)}, u32[]{:S(2)}) copy-start(bf16[32,32,1024]{2,1,0:T(8,128)(2,1)} %down_ref.1) | copy-start | bytes 6291460
  15.4 1.2 copy-start.9
  16.6 0.9 copy-start.10
  23.2 1.3 copy-start.3
  24.5 1.1 copy-start.4
  25.6 5.3 %copy-start.17 = (s32[1,16]{1,0:T(1,128)S(1)}, s32[1,16]{1,0:T(1,128)}, u32[]{:S(2)}) copy-start(s32[1,16]{1,0:T(1,128)} %param.19) | copy-start | bytes 196
  25.6 55.4 %all-to-all-start = ((bf16[32,32,1024]{2,1,0:T(8,128)(2,1)}), bf16[32,32,1024]{2,1,0:T(8,128)(2,1)}, u32[]{:S(2)}, u32[]{:S(2)}) async-start(bf16[32,32,1024]{2,1,0:T(8,128)(2,1)} %copy-done.3), calls=%async_computation | async-start | bytes 4194304 | tf_op jit(solution)/shard_map/all_to_all | solution.py:283
  80.9 35.4 %all-to-all-start.1 = ((bf16[32,16,1280]{2,1,0:T(8,128)(2,1)}), bf16[32,16,1280]{2,1,0:T(8,128)(2,1)S(1)}, u32[]{:S(2)}, u32[]{:S(2)}) async-start(bf16[32,16,1280]{2,1,0:T(8,128)(2,1)} %copy-done.4), calls=%async_computation.1 | async-start | bytes 2621440 | tf_op jit(solution)/shard_map/all_to_all | solution.py:283
  83.6 2.4 %copy-start.2 = (bf16[512,2048]{1,0:T(8,128)(2,1)S(1)}, bf16[512,2048]{1,0:T(8,128)(2,1)}, u32[]{:S(2)}) copy-start(bf16[512,2048]{1,0:T(8,128)(2,1)} %x_ref.1) | copy-start | bytes 6291460
  84.6 3.6 %copy-start.16 = (bf16[2048,512]{1,0:T(8,128)(2,1)S(1)}, bf16[2048,512]{1,0:T(8,128)(2,1)}, u32[]{:S(2)}) copy-start(bf16[2048,512]{1,0:T(8,128)(2,1)} %param.13) | copy-start | bytes 6291460
  86.0 4.5 %copy-start.15 = (bf16[2048,2048]{1,0:T(8,128)(2,1)S(1)}, bf16[2048,2048]{1,0:T(8,128)(2,1)}, u32[]{:S(2)}) copy-start(bf16[2048,2048]{1,0:T(8,128)(2,1)} %param.11) | copy-start | bytes 25165828
  99.6 0.7 copy-start.11
  100.3 0.7 copy-start.13
  116.5 1.2 copy-start.5
  117.7 1.2 copy-start.6
  118.9 0.9 copy-start.7
  119.9 0.9 copy-start.8
  120.8 0.9 copy-start.12
  121.8 0.9 copy-start.14

commit v3 on v2

--- a/solution.py
+++ b/solution.py
@@ -114,34 +114,146 @@
     )(pick, down, upq, upv)
 
 
-def low_kernel(x_ref, down_ref, owner_ref, lowq_ref, lowv_ref):
-    serves, stores, _, _, width = down_ref.shape
+def exchange_kernel(serves, stores, ups, *refs):
+    owner_ref, x_hbm, wq_hbm, wk_hbm, wv_hbm, *refs = refs
+    sends, refs = refs[: 1 + ups], refs[1 + ups :]
+    baseq_hbm, basek_hbm, basev_hbm, lowq_ref, lowv_ref, *refs = refs
+    ups_got, refs = refs[:ups], refs[ups:]
+    down_got, x_ref, wq_ref, wk_ref, wv_ref, baseq_ref, basek_ref, basev_ref, *sems = refs
+    send_sems, recv_sems, in_sems, out_sems = sems
+    gots = [down_got] + list(ups_got)
+    count = serves * stores
+    me = lax.axis_index("serve") * stores + lax.axis_index("store")
+
+    def peer(step):
+        there = lax.rem(me + step, count)
+        return there, (there // stores, lax.rem(there, stores))
+
+    def copy(which, step):
+        there, device = peer(step)
+        return pltpu.make_async_remote_copy(
+            src_ref=sends[which].at[there],
+            dst_ref=gots[which].at[me],
+            send_sem=send_sems.at[which, step],
+            recv_sem=recv_sems.at[which, step],
+            device_id=device,
+            device_id_type=pl.DeviceIdType.MESH,
+        )
+
+    loads = [
+        pltpu.make_async_copy(source, target, in_sems.at[i])
+        for i, (source, target) in enumerate(
+            [(x_hbm, x_ref), (wq_hbm, wq_ref), (wk_hbm, wk_ref), (wv_hbm, wv_ref)]
+        )
+    ]
+    for load in loads:
+        load.start()
+
+    barrier = pltpu.get_barrier_semaphore()
+
+    @pl.loop(1, count)
+    def _(step):
+        pl.semaphore_signal(
+            barrier, inc=1, device_id=peer(step)[1], device_id_type=pl.DeviceIdType.MESH
+        )
+
+    pl.semaphore_wait(barrier, count - 1)
+
+    for which in range(1 + ups):
+
+        @pl.loop(1, count)
+        def _(step):
+            copy(which, step).start()
+
+    for send, got in zip(sends, gots):
+        got[me] = send[me]
+
+    for load in loads:
+        load.wait()
+    stores_out = []
+    for i, (w_ref, base_ref, base_hbm) in enumerate(
+        [
+            (wq_ref, baseq_ref, baseq_hbm),
+            (wk_ref, basek_ref, basek_hbm),
+            (wv_ref, basev_ref, basev_hbm),
+        ]
+    ):
+        tile = min(256, w_ref.shape[1])
+
+        @pl.loop(0, w_ref.shape[1] // tile)
+        def _(c):
+            at = pl.ds(pl.multiple_of(c * tile, tile), tile)
+            base_ref[:, at] = jnp.dot(
+                x_ref[...], w_ref[:, at], preferred_element_type=jnp.float32
+            )
+
+        stores_out.append(pltpu.make_async_copy(base_ref, base_hbm, out_sems.at[i]))
+        stores_out[-1].start()
+
+    @pl.loop(1, count)
+    def _(step):
+        copy(0, step).wait_recv()
+
     rows = x_ref.shape[0]
+    width = down_got.shape[2]
     cols = stores * RANK
     mine = owner_ref[:, :1] == lax.broadcasted_iota(jnp.int32, (rows, cols), 1) // RANK
     for part, out_ref in enumerate((lowq_ref, lowv_ref)):
         total = jnp.zeros((rows, cols), jnp.float32)
         for s in range(serves):
+            panels = down_got[s * stores : (s + 1) * stores, part * RANK : (part + 1) * RANK, :]
             total += lax.dot_general(
                 x_ref[:, s * width : (s + 1) * width],
-                down_ref[s, :, part].reshape(cols, width),
+                panels.reshape(cols, width),
                 CONTRACT_LAST,
                 preferred_element_type=jnp.float32,
             )
         out_ref[...] = jnp.where(mine, total, 0.0).astype(jnp.bfloat16)
 
-
-def low_products(x, down, owner):
+    for which in range(1, 1 + ups):
+
+        @pl.loop(1, count)
+        def _(step):
+            copy(which, step).wait_recv()
+
+    for which in range(1 + ups):
+
+        @pl.loop(1, count)
+        def _(step):
+            copy(which, step).wait_send()
+
+    for store in stores_out:
+        store.wait()
+
+
+def exchange(owner, x, weights, sends, serves, stores):
+    count = serves * stores
     rows = x.shape[0]
-    cols = down.shape[1] * RANK
+    ups = len(sends) - 1
+    anywhere = pl.BlockSpec(memory_space=pl.ANY)
+    bases = [(rows, w.shape[1]) for w in weights]
+    low = jax.ShapeDtypeStruct((rows, stores * RANK), jnp.bfloat16)
     return pl.pallas_call(
-        low_kernel,
-        out_shape=[jax.ShapeDtypeStruct((rows, cols), jnp.bfloat16)] * 2,
-        in_specs=[VMEM] * 3,
-        out_specs=[VMEM] * 2,
-        compiler_params=pltpu.CompilerParams(vmem_limit_bytes=32 << 20),
-        name="low",
-    )(x, down, owner)
+        functools.partial(exchange_kernel, serves, stores, ups),
+        out_shape=[jax.ShapeDtypeStruct(base, jnp.float32) for base in bases]
+        + [low, low]
+        + [jax.ShapeDtypeStruct(a.shape, a.dtype) for a in sends[1:]],
+        in_specs=[VMEM] + [anywhere] * 4 + [VMEM] * len(sends),
+        out_specs=[anywhere] * 3 + [VMEM] * (2 + ups),
+        scratch_shapes=[pltpu.VMEM(sends[0].shape, sends[0].dtype), pltpu.VMEM(x.shape, x.dtype)]
+        + [pltpu.VMEM(w.shape, w.dtype) for w in weights]
+        + [pltpu.VMEM(base, jnp.float32) for base in bases]
+        + [
+            pltpu.SemaphoreType.DMA((1 + ups, count)),
+            pltpu.SemaphoreType.DMA((1 + ups, count)),
+            pltpu.SemaphoreType.DMA((4,)),
+            pltpu.SemaphoreType.DMA((3,)),
+        ],
+        compiler_params=pltpu.CompilerParams(
+            collective_id=1, has_side_effects=True, vmem_limit_bytes=56 << 20
+        ),
+        name="exchange",
+    )(owner, x, *weights, *sends)
 
 
 def turned(x, cos, sin):
@@ -252,7 +364,7 @@
             whole(pos),
         ],
         out_specs=block(wide),
-        compiler_params=pltpu.CompilerParams(vmem_limit_bytes=48 << 20),
+        compiler_params=pltpu.CompilerParams(vmem_limit_bytes=60 << 20),
         name="attend",
     )(baseq, basek, basev, lowq, lowv, upq, upv, cos, sin, pos)
 
@@ -279,13 +391,7 @@
     pick = jnp.sum(jnp.where(lanes[None, :] == my_store, all_asked, 0), axis=1)
     joined = upv.shape[2] % LANES == 0
 
-    def exchange(a):
-        return lax.all_to_all(a, axes, split_axis=0, concat_axis=0, tiled=True)
-
-    down_got, *up_got = [exchange(a) for a in choose(pick, down, upq, upv, joined)]
-    down_got = down_got.reshape(serves, stores, 2, RANK, down.shape[2])
-    up_got = [a.reshape((serves, stores) + a.shape[1:]) for a in up_got]
-    upq_got, upv_got = up_got[0], up_got[-1]
+    sends = choose(pick, down, upq, upv, joined)
 
     order = jnp.arange(requests, dtype=jnp.int32)
     ends = jnp.sum(jnp.where(order[None, :] <= order[:, None], lengths[None, :], 0), axis=1)
@@ -303,10 +409,11 @@
     pos = jnp.broadcast_to(positions[:, None], (rows, LANES))
     owner = jnp.broadcast_to(owner[:, None], (rows, LANES))
 
-    baseq = jnp.dot(x, wq, preferred_element_type=jnp.float32)
-    basek = jnp.dot(x, wk, preferred_element_type=jnp.float32)
-    basev = jnp.dot(x, wv, preferred_element_type=jnp.float32)
-    lowq, lowv = low_products(x, down_got, owner)
+    baseq, basek, basev, lowq, lowv, *up_got = exchange(
+        owner, x, (wq, wk, wv), sends, serves, stores
+    )
+    up_got = [a.reshape((serves, stores) + a.shape[1:]) for a in up_got]
+    upq_got, upv_got = up_got[0], up_got[-1]
     return attend(baseq, basek, basev, lowq, lowv, upq_got, upv_got, cos, sin, pos, serves, joined)
 
 

time: 139 us -> 130 us (0.935)
  the two profiles are of different devices: /device:TPU:0 before, /device:TPU:15 now
where the time goes in v3:
time: 130 us; the launch traced here: 128 us
  Pallas kernels  114 us (88%)
  local copies, waits for them, and re-layouts  8.39 us (6%)
  other arithmetic  5.66 us (4%)
    pallas_call x1, Pallas kernels, exchange(): pl.pallas_call(functools.partial(exchange_kernel, serves, stores, ups), o...  83.4 us
    pallas_call x1, Pallas kernels, attend(): pl.pallas_call(attend_kernel, out_shape=jax.ShapeDtypeStruct((rows, width...  15.9 us
    pallas_call x1, Pallas kernels, ask(): pl.pallas_call(functools.partial(ask_kernel, serves, stores), out_shape=j...  9.29 us
    unnamed x10, local copies, waits for them, and re-layouts  6.18 us
    pallas_call x1, Pallas kernels, choose(): pl.pallas_call(functools.partial(choose_kernel, joined), out_shape=[jax.S...  5.55 us

profile of v3, /device:TPU:15, one launch (start us, length us, event | category | flops | bytes accessed | tf_op | source)
XLA Modules:
  0.0 128.3 jit_solution(8649545445894652307)
XLA Ops:
  0.0 0.8 select_reduce_fusion.5
  0.8 0.7 fusion.2
  1.4 0.9 select_reduce_fusion.2
  2.3 0.1 select_reduce_fusion
  2.4 0.8 broadcast_in_dim.98.refs_0_
  3.3 0.1 select_reduce_fusion.4
  3.4 0.5 pad_bitcast_fusion.asked_ref
  3.9 9.3 %ask.1 = s32[32,1,128]{2,1,0:T(1,128)} custom-call(s32[1,128]{1,0:T(1,128)} %pad_bitcast_fusion.asked_ref), custom_call_target="tpu_custom_call" | custom-call | tf_op jit(solution)/shard_map/ask/pallas_call | solution.py:61
  13.2 0.8 select_reduce_fusion.3.pick_ref
  14.0 0.0 copy-start.1
  14.0 1.6 %copy-done.1 = bf16[32,32,1024]{2,1,0:T(8,128)(2,1)S(1)} copy-done((bf16[32,32,1024]{2,1,0:T(8,128)(2,1)S(1)}, bf16[32,32,1024]{2,1,0:T(8,128)(2,1)}, u32[]{:S(2)}) %copy-start.1) | copy-done | bytes 2097176
  15.6 0.0 copy-start.3
  15.6 1.2 copy-done.3
  16.9 0.0 copy-start.4
  16.9 0.9 copy-done.4
  17.8 5.6 %choose.1 = (bf16[32,32,1024]{2,1,0:T(8,128)(2,1)S(1)}, bf16[32,16,1280]{2,1,0:T(8,128)(2,1)S(1)}) custom-call(s32[32]{0:T(128)S(1)} %select_reduce_fusion.3.pick_ref, bf16[32,32,1024]{2,1,0:T(8,128)(2,1)S(1)} %copy-done.1, bf16[32,16,1024]{2,1,0:T(8,128)(2,1)S(1)} %copy-done.3, bf16[32,16,256]{2,1,0:T(8,128)(2,1)S(1)} %copy-done.4), custom_call_target="tpu_custom_call" | custom-call | tf_op jit(solution)/shard_map/choose/pallas_call | solution.py:106
  23.4 0.0 copy-start
  23.4 1.3 %copy-done = bf16[32,32,1024]{2,1,0:T(8,128)(2,1)} copy-done((bf16[32,32,1024]{2,1,0:T(8,128)(2,1)}, bf16[32,32,1024]{2,1,0:T(8,128)(2,1)S(1)}, u32[]{:S(2)}) %copy-start) | copy-done | bytes 2097176
  24.7 1.1 copy-done.2
  25.8 83.4 %exchange.1 = (f32[512,2048]{1,0:T(8,128)}, f32[512,512]{1,0:T(8,128)}, f32[512,512]{1,0:T(8,128)}, bf16[512,256]{1,0:T(8,128)(2,1)}, bf16[512,256]{1,0:T(8,128)(2,1)}, /*index=5*/bf16[32,16,1280]{2,1,0:T(8,128)(2,1)}) custom-call(s32[512,128]{1,0:T(8,128)} %broadcast_in_dim.98.refs_0_, bf16[512,2048]{1,0:T(8,128)(2,1)} %refs_1_.1, ...), custom_call_target="tpu_custom_call" | custom-call | tf_op jit(solution)/shard_map/exchange/pallas_call | solution.py:236
  109.2 1.0 fusion
  110.2 1.3 %pad_maximum_fusion = (f32[512,128]{1,0:T(8,128)}, f32[512,128]{1,0:T(8,128)}) fusion(f32[512,32]{1,0:T(8,128)S(1)} %get-tuple-element.25, f32[512,32]{1,0:T(8,128)S(1)} %get-tuple-element.24, f32[512,32]{1,0:T(8,128)S(1)} %get-tuple-element.23), kind=kLoop, calls=%fused_computation.2 | loop fusion | flops 393216 | bytes 720896 | tf_op jit(solution)/shard_map/concatenate | solution.py:407
  111.5 0.8 broadcast_in_dim.103.pos_ref
  112.3 15.9 %attend.1 = bf16[512,2048]{1,0:T(8,128)(2,1)} custom-call(f32[512,2048]{1,0:T(8,128)} %get-tuple-element.15.baseq_ref, f32[512,512]{1,0:T(8,128)} %get-tuple-element.16.basek_ref, f32[512,512]{1,0:T(8,128)} %get-tuple-element.17.basev_ref, bf16[512,256]{1,0:T(8,128)(2,1)} %get-tuple-element.18.lowq_ref, bf16[512,256]{1,0:T(8,128)(2,1)} %get-tuple-element.19.lowv_ref, ...), custom_call_target="tpu_custom_call" | custom-call | tf_op jit(solution)/shard_map/attend/pallas_call | solution.py:350
  (5 shorter events, 0.0 us)
Async XLA Ops:
  14.0 1.6 %copy-start.1 = (bf16[32,32,1024]{2,1,0:T(8,128)(2,1)S(1)}, bf16[32,32,1024]{2,1,0:T(8,128)(2,1)}, u32[]{:S(2)}) copy-start(bf16[32,32,1024]{2,1,0:T(8,128)(2,1)} %down_ref.1) | copy-start | bytes 6291460
  15.6 1.2 copy-start.3
  16.9 0.9 copy-start.4
  23.4 1.3 %copy-start = (bf16[32,32,1024]{2,1,0:T(8,128)(2,1)}, bf16[32,32,1024]{2,1,0:T(8,128)(2,1)S(1)}, u32[]{:S(2)}) copy-start(bf16[32,32,1024]{2,1,0:T(8,128)(2,1)S(1)} %get-tuple-element.13.refs_5_) | copy-start | bytes 6291460
  24.7 1.1 copy-start.2

commit v4 on v3

--- a/solution.py
+++ b/solution.py
@@ -109,7 +109,7 @@
         in_specs=[pl.BlockSpec(memory_space=pltpu.SMEM)] + [anywhere] * 3,
         out_specs=[VMEM] * len(shapes),
         scratch_shapes=[pltpu.SemaphoreType.DMA((3, count))],
-        compiler_params=pltpu.CompilerParams(vmem_limit_bytes=32 << 20),
+        compiler_params=pltpu.CompilerParams(vmem_limit_bytes=60 << 20),
         name="choose",
     )(pick, down, upq, upv)
 

time: 130 us -> 124 us (0.954)
  local copies, waits for them, and re-layouts: 8.39 us -> 2.22 us
    unnamed x10 -> x0, local copies, waits for them, and re-layouts: 6.18 us -> none
where the time goes in v4:
time: 124 us; the launch traced here: 122 us
  Pallas kernels  114 us (92%)
  other arithmetic  6.24 us (5%)
  local copies, waits for them, and re-layouts  2.22 us (2%)
    pallas_call x1, Pallas kernels, exchange(): pl.pallas_call(functools.partial(exchange_kernel, serves, stores, ups), o...  83.4 us
    pallas_call x1, Pallas kernels, attend(): pl.pallas_call(attend_kernel, out_shape=jax.ShapeDtypeStruct((rows, width...  15.9 us
    pallas_call x1, Pallas kernels, ask(): pl.pallas_call(functools.partial(ask_kernel, serves, stores), out_shape=j...  9.29 us
    pallas_call x1, Pallas kernels, choose(): pl.pallas_call(functools.partial(choose_kernel, joined), out_shape=[jax.S...  5.38 us

profile of v4, /device:TPU:15, one launch (start us, length us, event | category | flops | bytes accessed | tf_op | source)
XLA Modules:
  0.0 122.5 jit_solution(5579038514552819160)
XLA Ops:
  0.0 0.8 select_reduce_fusion.5
  0.8 0.7 fusion.2
  1.4 0.9 select_reduce_fusion.2
  2.3 0.1 select_reduce_fusion
  2.4 0.9 broadcast_in_dim.98.refs_0_
  3.3 0.1 select_reduce_fusion.4
  3.4 0.5 pad_bitcast_fusion.asked_ref
  3.9 9.3 %ask.1 = s32[32,1,128]{2,1,0:T(1,128)} custom-call(s32[1,128]{1,0:T(1,128)} %pad_bitcast_fusion.asked_ref), custom_call_target="tpu_custom_call" | custom-call | tf_op jit(solution)/shard_map/ask/pallas_call | solution.py:61
  13.2 1.4 %select_reduce_fusion.3.pick_ref = s32[32]{0:T(128)} fusion(s32[32,128]{1,0:T(8,128)} %bitcast.14, pred[128]{0:T(512)(128)(4,1)S(1)} %iota_compare_fusion.5), kind=kLoop, calls=%fused_computation.12 | loop fusion | flops 8160 | bytes 16640 | tf_op jit(solution)/shard_map/reduce_sum | solution.py:391
  14.6 5.4 %choose.1 = (bf16[32,32,1024]{2,1,0:T(8,128)(2,1)}, bf16[32,16,1280]{2,1,0:T(8,128)(2,1)}) custom-call(s32[32]{0:T(128)} %select_reduce_fusion.3.pick_ref, bf16[32,32,1024]{2,1,0:T(8,128)(2,1)} %down_ref.1, bf16[32,16,1024]{2,1,0:T(8,128)(2,1)} %upq_ref.1, bf16[32,16,256]{2,1,0:T(8,128)(2,1)} %upv_ref.1), custom_call_target="tpu_custom_call" | custom-call | tf_op jit(solution)/shard_map/choose/pallas_call | solution.py:106
  20.0 83.4 %exchange.1 = (f32[512,2048]{1,0:T(8,128)}, f32[512,512]{1,0:T(8,128)}, f32[512,512]{1,0:T(8,128)}, bf16[512,256]{1,0:T(8,128)(2,1)}, bf16[512,256]{1,0:T(8,128)(2,1)}, /*index=5*/bf16[32,16,1280]{2,1,0:T(8,128)(2,1)}) custom-call(s32[512,128]{1,0:T(8,128)} %broadcast_in_dim.98.refs_0_, bf16[512,2048]{1,0:T(8,128)(2,1)} %refs_1_.1, ...), custom_call_target="tpu_custom_call" | custom-call | tf_op jit(solution)/shard_map/exchange/pallas_call | solution.py:236
  103.4 1.0 fusion
  104.4 1.3 %pad_maximum_fusion = (f32[512,128]{1,0:T(8,128)}, f32[512,128]{1,0:T(8,128)}) fusion(f32[512,32]{1,0:T(8,128)S(1)} %get-tuple-element.25, f32[512,32]{1,0:T(8,128)S(1)} %get-tuple-element.24, f32[512,32]{1,0:T(8,128)S(1)} %get-tuple-element.23), kind=kLoop, calls=%fused_computation.2 | loop fusion | flops 393216 | bytes 720896 | tf_op jit(solution)/shard_map/concatenate | solution.py:407
  105.7 0.8 broadcast_in_dim.103.pos_ref
  106.5 15.9 %attend.1 = bf16[512,2048]{1,0:T(8,128)(2,1)} custom-call(f32[512,2048]{1,0:T(8,128)} %get-tuple-element.15.baseq_ref, f32[512,512]{1,0:T(8,128)} %get-tuple-element.16.basek_ref, f32[512,512]{1,0:T(8,128)} %get-tuple-element.17.basev_ref, bf16[512,256]{1,0:T(8,128)(2,1)} %get-tuple-element.18.lowq_ref, bf16[512,256]{1,0:T(8,128)(2,1)} %get-tuple-element.19.lowv_ref, ...), custom_call_target="tpu_custom_call" | custom-call | tf_op jit(solution)/shard_map/attend/pallas_call | solution.py:350
  (4 shorter events, 0.0 us)
